TPU v7x, 128 devices: a whole 4x4x4 slice. The times are simulated.
128 devices in a mesh: proto: 32 (over z, x, core), rows: 4 (over y).
Axes of the slice: x: 4, y: 4, z: 4, core: 2. Of those that a mesh axis runs over, the one named last changes fastest.
Arguments:
- student_patches: bfloat16 [8192, 256], P('rows'), may hold values from -8 to 8
- teacher_patches: bfloat16 [8192, 256], P('rows'), may hold values from -8 to 8
- mask_index: int32 [4096], P('rows'), may hold values from 0 to 2047
- proto_weight: bfloat16 [131072, 256], P('proto'), may hold values from -1 to 1
- row_cotangent: float32 [4096], P('rows'), may hold values from -6 to 6
Outputs:
- loss: float32 [4096], P('rows')
- grad_patches: float32 [8192, 256], P('rows')
- grad_weight: float32 [131072, 256], P(('proto', 'rows'))
Inputs may be any that keep to these rules, and one draw needn't show every extreme that they name: Each entry names one of the 2048 patches of its own row group: row i uses patch (i // 1024) * 2048 + mask_index[i]; entries may repeat.
All inputs are finite; a program needn't handle non-finite values.
Results may differ from a plain program's by a relative error of at most 0.023.
Values may be sent and summed in bfloat16 or wider, within the bound.
A program may use at most 128 MiB of HBM per device.

v0:
```python
import jax
import jax.numpy as jnp
from jax import lax
from jax.sharding import PartitionSpec as P

SWEEPS = 3


teacher_temp = 0.07
student_temp = 0.1
epsilon = 1e-06


def unit_rows(values):
    scale_rows = lax.rsqrt(jnp.sum(values * values, axis=1, keepdims=True) + epsilon)
    return (values * scale_rows, scale_rows)


def contract_last(left_side, right_side):
    return lax.dot_general(
        left_side, right_side, (((1,), (1,)), ((), ())), preferred_element_type=jnp.float32
    )


def unit_backward(unit_value, scale_rows, grad_value):
    return (
        grad_value - unit_value * jnp.sum(unit_value * grad_value, axis=1, keepdims=True)
    ) * scale_rows


def shards(student_patches, teacher_patches, mask_index, proto_weight, row_cotangent):
    local_rows = mask_index.shape[0]
    local_protos = proto_weight.shape[0]
    all_rows = float(local_rows * lax.axis_size("rows"))
    all_protos = float(local_protos * lax.axis_size("proto"))
    student_unit, student_scale = unit_rows(
        jnp.take(student_patches, mask_index, axis=0).astype(jnp.float32)
    )
    student_half = student_unit.astype(jnp.bfloat16)
    teacher_unit, teacher_scale = unit_rows(
        jnp.take(teacher_patches, mask_index, axis=0).astype(jnp.float32)
    )
    teacher_half = teacher_unit.astype(jnp.bfloat16)
    weight_unit, weight_scale = unit_rows(proto_weight.astype(jnp.float32))
    weight_half = weight_unit.astype(jnp.bfloat16)
    transport = jnp.exp(contract_last(teacher_half, weight_half) / teacher_temp)
    student_logits = contract_last(student_half, weight_half) / student_temp
    student_expo = jnp.exp(student_logits)
    for repeat in range(SWEEPS):
        column_totals = lax.psum(jnp.sum(transport, axis=0), "rows")
        current = transport / (column_totals[None, :] * all_protos)
        totals = lax.psum(jnp.sum(current, axis=1), "proto")
        transport = current / (totals[:, None] * all_rows)
    targets = transport * all_rows
    expo_total, cross = lax.psum(
        (jnp.sum(student_expo, axis=1), jnp.sum(targets * student_logits, axis=1)), "proto"
    )
    loss = jnp.log(expo_total) - cross
    student_probs = student_expo / expo_total[:, None]
    grad_scores = (row_cotangent[:, None] * (student_probs - targets) / student_temp).astype(
        jnp.bfloat16
    )
    grad_unit = lax.psum(
        jnp.dot(grad_scores, weight_half, preferred_element_type=jnp.float32).astype(jnp.bfloat16),
        "proto",
    ).astype(jnp.float32)
    grad_rows = unit_backward(student_unit, student_scale, grad_unit)
    grad_patches = (
        jnp.zeros((student_patches.shape[0], student_patches.shape[1]), jnp.float32)
        .at[mask_index]
        .add(grad_rows)
    )
    keep_protos = local_protos // lax.axis_size("rows")
    grad_weight_unit = lax.psum_scatter(
        lax.dot_general(
            grad_scores, student_half, (((0,), (0,)), ((), ())), preferred_element_type=jnp.float32
        ).astype(jnp.bfloat16),
        "rows",
        scatter_dimension=0,
        tiled=True,
    ).astype(jnp.float32)
    begin_proto = lax.axis_index("rows") * keep_protos
    unit_keep = lax.dynamic_slice_in_dim(weight_unit, begin_proto, keep_protos, 0)
    scale_keep = lax.dynamic_slice_in_dim(weight_scale, begin_proto, keep_protos, 0)
    grad_weight = unit_backward(unit_keep, scale_keep, grad_weight_unit)
    return (loss, grad_patches, grad_weight)


def solution(mesh):
    in_specs = (P("rows", None), P("rows", None), P("rows"), P("proto", None), P("rows"))
    out_specs = (P("rows"), P("rows", None), P(("proto", "rows"), None))
    return jax.shard_map(shards, mesh=mesh, in_specs=in_specs, out_specs=out_specs, check_vma=False)
```

profile of v0, /device:TPU:1, one launch (start us, length us, event | category | flops | bytes accessed | tf_op | source)
XLA Modules:
  0.0 528.8 jit_solution(8387681722513930330)
XLA Ops:
  8.1 0.8 compare_select_fusion
  8.8 0.7 compare_and_fusion
  9.5 2.2 fusion.12
  11.8 3.9 gather_fusion.1
  15.7 4.8 gather_fusion
  20.6 0.7 fusion.16
  21.3 8.7 %fusion.36 = (f32[4096]{0:T(1024)S(1)}, f32[1024,4096]{1,0:T(8,128)}) fusion(f32[4096]{0:T(1024)S(1)} %add_rsqrt_fusion, bf16[4096,256]{1,0:T(8,128)(2,1)} %param.10, f32[1024]{0:T(1024)S(1)} %add_rsqrt_fusion.1, bf16[1024,256]{1,0:T(8,128)(2,1)S(1)} %gather_fusion.1, pred[1024]{0:T(1024)(128)(4,1)S(1)} %compare_and_fusion), kind=kOutput, calls=%fused_computation.69 | convolution fusion | flops 2160062464 | bytes 19436544 | tf_op jit(solution)/shard_map/dot_general | solution.py:20
  29.9 14.2 %psum.64 = f32[4096]{0:T(1024)S(1)} all-reduce(f32[4096]{0:T(1024)S(1)} %get-tuple-element.12), channel_id=1, replica_groups=mesh['proto'=32,'rows'=4] {'rows'}, use_global_device_ids=true, to_apply=%region_6.8 | all-reduce | flops 4096 | bytes 32768 | tf_op jit(solution)/shard_map/psum | solution.py:50
  44.2 6.9 %divide_reduce_fusion = f32[1024]{0:T(1024)S(1)} fusion(f32[1024,4096]{1,0:T(8,128)} %get-tuple-element.13, f32[4096]{0:T(1024)S(1)} %broadcast_multiply_fusion.2), kind=kLoop, calls=%fused_computation.16 | loop fusion | flops 8387584 | bytes 16797696 | tf_op jit(solution)/shard_map/reduce_sum | solution.py:52
  51.1 67.8 %psum.65 = f32[1024]{0:T(1024)S(1)} all-reduce(f32[1024]{0:T(1024)S(1)} %divide_reduce_fusion), channel_id=1, replica_groups=mesh['proto'=32,'rows'=4] {'proto'}, use_global_device_ids=true, to_apply=%region_8.10 | all-reduce | flops 1024 | bytes 8192 | tf_op jit(solution)/shard_map/psum | solution.py:52
  118.9 8.1 %fusion.8 = f32[4096]{0:T(1024)S(1)} fusion(f32[1024,4096]{1,0:T(8,128)} %get-tuple-element.13, f32[1024]{0:T(1024)S(1)} %broadcast_multiply_fusion.5, f32[4096]{0:T(1024)S(1)} %broadcast_multiply_fusion.2), kind=kLoop, calls=%fused_computation.17 | loop fusion | flops 12578816 | bytes 16814080 | tf_op jit(solution)/shard_map/reduce_sum | solution.py:50
  127.0 10.8 %psum.66 = f32[4096]{0:T(1024)S(1)} all-reduce(f32[4096]{0:T(1024)S(1)} %fusion.8), channel_id=1, replica_groups=mesh['proto'=32,'rows'=4] {'rows'}, use_global_device_ids=true, to_apply=%region_10.12 | all-reduce | flops 4096 | bytes 32768 | tf_op jit(solution)/shard_map/psum | solution.py:50
  137.8 7.6 %fusion.9 = f32[1024]{0:T(1024)S(1)} fusion(f32[1024,4096]{1,0:T(8,128)} %get-tuple-element.13, f32[4096]{0:T(1024)S(1)} %broadcast_multiply_fusion.1, f32[1024]{0:T(1024)S(1)} %broadcast_multiply_fusion.5, f32[4096]{0:T(1024)S(1)} %broadcast_multiply_fusion.2), kind=kLoop, calls=%fused_computation.18 | loop fusion | flops 16776192 | bytes 16818176 | tf_op jit(solution)/shard_map/reduce_sum | solution.py:52
  145.4 66.8 %psum.67 = f32[1024]{0:T(1024)S(1)} all-reduce(f32[1024]{0:T(1024)S(1)} %fusion.9), channel_id=1, replica_groups=mesh['proto'=32,'rows'=4] {'proto'}, use_global_device_ids=true, to_apply=%region_12.14 | all-reduce | flops 1024 | bytes 8192 | tf_op jit(solution)/shard_map/psum | solution.py:52
  212.2 8.0 %fusion.10 = f32[4096]{0:T(1024)S(1)} fusion(f32[1024,4096]{1,0:T(8,128)} %get-tuple-element.13, f32[1024]{0:T(1024)S(1)} %broadcast_multiply_fusion.4, f32[4096]{0:T(1024)S(1)} %broadcast_multiply_fusion.1, f32[1024]{0:T(1024)S(1)} %broadcast_multiply_fusion.5, f32[4096]{0:T(1024)S(1)} %broadcast_multiply_fusion.2), kind=kLoop, calls=%fused_computation.19 | loop fusion | flops 20967424 | bytes 16834560 | tf_op jit(solution)/shard_map/reduce_sum | solution.py:50
  220.2 11.7 %psum.68 = f32[4096]{0:T(1024)S(1)} all-reduce(f32[4096]{0:T(1024)S(1)} %fusion.10), channel_id=1, replica_groups=mesh['proto'=32,'rows'=4] {'rows'}, use_global_device_ids=true, to_apply=%region_14.16 | all-reduce | flops 4096 | bytes 32768 | tf_op jit(solution)/shard_map/psum | solution.py:50
  231.9 8.2 %fusion.11 = f32[1024]{0:T(1024)S(1)} fusion(f32[1024,4096]{1,0:T(8,128)} %get-tuple-element.13, f32[4096]{0:T(1024)S(1)} %broadcast_multiply_fusion, f32[1024]{0:T(1024)S(1)} %broadcast_multiply_fusion.4, f32[4096]{0:T(1024)S(1)} %broadcast_multiply_fusion.1, f32[1024]{0:T(1024)S(1)} %broadcast_multiply_fusion.5, f32[4096]{0:T(1024)S(1)} %broadcast_multiply_fusion.2), kind=kLoop, calls=%fused_computation.20 | loop fusion | flops 25164800 | bytes 16838656 | tf_op jit(solution)/shard_map/reduce_sum | solution.py:52
  240.1 66.4 %psum.69 = f32[1024]{0:T(1024)S(1)} all-reduce(f32[1024]{0:T(1024)S(1)} %fusion.11), channel_id=1, replica_groups=mesh['proto'=32,'rows'=4] {'proto'}, use_global_device_ids=true, to_apply=%region_16.18 | all-reduce | flops 1024 | bytes 8192 | tf_op jit(solution)/shard_map/psum | solution.py:52
  306.5 16.9 %exponential_reduce_fusion = (f32[1024]{0:T(1024)S(1)}, f32[1024]{0:T(1024)S(1)}, f32[1024,4096]{1,0:T(8,128)}) fusion(f32[1024,4096]{1,0:T(8,128)} %get-tuple-element.13, f32[1024]{0:T(1024)S(1)} %broadcast_multiply_fusion.3, f32[4096]{0:T(1024)S(1)} %broadcast_multiply_fusion, f32[1024]{0:T(1024)S(1)} %broadcast_multiply_fusion.4, ...), kind=kOutput, calls=%fused_computation.21 | convolution fusion | flops 2197813248 | bytes 36267008 | tf_op jit(solution)/shard_map/dot_general | solution.py:20
  323.5 63.6 %all-reduce = (f32[1024]{0:T(1024)S(1)}, f32[1024]{0:T(1024)S(1)}) all-reduce(f32[1024]{0:T(1024)S(1)} %get-tuple-element.5, f32[1024]{0:T(1024)S(1)} %get-tuple-element.4), channel_id=1, replica_groups=mesh['proto'=32,'rows'=4] {'proto'}, use_global_device_ids=true, to_apply=%region_18.20 | all-reduce | flops 2048 | bytes 16384 | tf_op jit(solution)/shard_map/psum | solution.py:55
  387.1 15.0 %multiply_convert_fusion = bf16[1024,4096]{1,0:T(8,128)(2,1)S(1)} fusion(f32[1024,4096]{1,0:T(8,128)} %get-tuple-element.14, f32[1024]{0:T(1024)S(1)} %get-tuple-element.9, f32[1024]{0:T(1024)S(1)} %copy-done.4, f32[1024,4096]{1,0:T(8,128)} %get-tuple-element.13, f32[1024]{0:T(1024)S(1)} %broadcast_multiply_fusion.3, f32[4096]{0:T(1024)S(1)} %broadcast_multiply_fusion, ...), kind=kLoop, calls=%fused_computation.13 | loop fusion | flops 54525952 | bytes 42012672 | tf_op jit(solution)/shard_map/convert_element_type | solution.py:60
  402.2 3.2 copy-done.3
  405.4 3.3 convolution_convert_fusion.1
  408.7 0.3 reduce-scatter.2.cloned.1.call-start
  409.0 7.7 %convolution_convert_fusion = bf16[4096,256]{1,0:T(8,128)(2,1)} fusion(bf16[1024,4096]{1,0:T(8,128)(2,1)} %copy-done.3, f32[1024]{0:T(1024)S(1)} %add_rsqrt_fusion.2, bf16[1024,256]{1,0:T(8,128)(2,1)} %copy-done.2, pred[1024]{0:T(1024)(128)(4,1)S(1)} %compare_and_fusion), kind=kOutput, calls=%fused_computation.24 | convolution fusion | flops 2149580800 | bytes 11015168 | tf_op jit(solution)/shard_map/dot_general | solution.py:75
  416.7 0.6 log_subtract_fusion
  417.3 2.3 convert_multiply_fusion
  419.6 87.5 %all-reduce.3.cloned.1.call-done = bf16[1024,256]{1,0:T(8,128)(2,1)} async-done(((bf16[1024,256]{1,0:T(8,128)(2,1)}), bf16[1024,256]{1,0:T(8,128)(2,1)}) %all-reduce.3.cloned.1.call-update) | async-done | bytes 524304 | tf_op jit(solution)/shard_map/psum | solution.py:63
  507.1 1.7 fusion.18
  508.8 8.2 %scatter_custom_fusion = f32[2048,256]{1,0:T(8,128)} fusion(s32[1024]{0:T(1024)S(1)} %get-tuple-element.10, bf16[1024,256]{1,0:T(8,128)(2,1)} %all-reduce.3.cloned.1.call-done, f32[]{:T(128)} %constant.19.clone.1, f32[1024]{0:T(1024)S(1)} %fusion.18, f32[1024]{0:T(1024)S(1)} %add_rsqrt_fusion.2, bf16[1024,256]{1,0:T(8,128)(2,1)} %copy-done.2, ...), kind=kCustom, calls=%fused_computation.42 | custom fusion | flops 2097152 | bytes 3154948 | tf_op jit(solution)/shard_map/scatter-add | solution.py:71
  517.0 1.6 fusion.22
  518.6 2.7 fusion.23
  (23 shorter events, 0.2 us)
Async XLA Ops:
  8.0 3.8 copy-start
  8.0 499.1 %all-reduce.3.cloned.1.call-start = ((), (), s32[]{:S(2)}) async-start(), calls=%async_computation.1 | async-start | bytes 1048576 | tf_op jit(solution)/shard_map/psum | solution.py:63
  20.5 30.6 %copy-start.2 = (bf16[1024,256]{1,0:T(8,128)(2,1)}, bf16[1024,256]{1,0:T(8,128)(2,1)S(1)}, u32[]{:S(2)}) copy-start(bf16[1024,256]{1,0:T(8,128)(2,1)S(1)} %gather_fusion) | copy-start | bytes 1572868
  212.2 94.3 %copy-start.1 = (bf16[4096,256]{1,0:T(8,128)(2,1)S(1)}, bf16[4096,256]{1,0:T(8,128)(2,1)}, u32[]{:S(2)}) copy-start(bf16[4096,256]{1,0:T(8,128)(2,1)} %param.10) | copy-start | bytes 6291460
  306.5 80.6 %copy-start.4 = (f32[1024]{0:T(1024)S(1)}, f32[1024]{0:T(1024)}, u32[]{:S(2)}) copy-start(f32[1024]{0:T(1024)} %param.11) | copy-start | bytes 12292
  402.2 3.2 copy-start.3
  408.7 108.3 %reduce-scatter.2.cloned.1.call-start = ((), (), s32[]{:S(2)}) async-start(), calls=%async_computation.2 | async-start | bytes 2621440 | tf_op jit(solution)/shard_map/reduce_scatter | solution.py:74
Sparse Core Ops, SparseCore 0:
  408.8 98.2 all-reduce.2
Sparse Core Ops, SparseCore 1:
  416.8 23.6 reduce-scatter.1
where the time goes:
time: 529 us
  blocking collectives  301 us (57%)
  waiting for transfers between devices  87.5 us (17%)
  other arithmetic  75.5 us (14%)
  matrix products  36.6 us (7%)
  between operations  15.6 us (3%)
  local copies, waits for them, and re-layouts  12 us (2%)
    psum x3, blocking collectives, shards(): totals = lax.psum(jnp.sum(current, axis=1), 'proto')  201 us
    psum x1, waiting for transfers between devices, shards(): lax.psum(jnp.dot(grad_scores, weight_half, preferred_element_type=jnp.flo...  87.5 us
    psum x1, blocking collectives, shards(): lax.psum((jnp.sum(student_expo, axis=1), jnp.sum(targets * student_logits...  63.6 us
    psum x3, blocking collectives, shards(): column_totals = lax.psum(jnp.sum(transport, axis=0), 'rows')  36.7 us
    dot_general x2, matrix products, contract_last(): lax.dot_general(left_side, right_side, (((1,), (1,)), ((), ())), preferre...  25.6 us
    reduce_sum x3, other arithmetic, shards(): totals = lax.psum(jnp.sum(current, axis=1), 'proto')  22.7 us
    reduce_sum x2, other arithmetic, shards(): column_totals = lax.psum(jnp.sum(transport, axis=0), 'rows')  16.1 us
    convert_element_type x1, other arithmetic, shards(): (row_cotangent[:, None] * (student_probs - targets) / student_temp).astyp...  15 us
  transfers between devices with their start and end apart: 2, of which 1 were waited for; matrix products, arithmetic and copies ran while one was open for 4% of the time, Pallas kernels for 0%

commit v1 on v0

v1 whole, which is shorter than its diff:
```python
import jax
import jax.numpy as jnp
from jax import lax
from jax.experimental import pallas as pl
from jax.experimental.pallas import tpu as pltpu
from jax.sharding import PartitionSpec as P

teacher_temp = 0.07
student_temp = 0.1
epsilon = 1e-06

f32, bf16 = jnp.float32, jnp.bfloat16
MESH = pl.DeviceIdType.MESH
NN = (((1,), (0,)), ((), ()))
NT = (((1,), (1,)), ((), ()))
TN = (((0,), (0,)), ((), ()))

D = 256
LANES = 128
BLOCK = 256
WIDE = 512


def dot(left, right, dims):
    return lax.dot_general(left, right, dims, preferred_element_type=f32)


def fold(row):
    count = row.shape[1] // LANES
    return jnp.concatenate([row[:, i * LANES : (i + 1) * LANES] for i in range(count)], axis=0)


def unfold(square):
    return jnp.concatenate([square[i : i + 1, :] for i in range(square.shape[0])], axis=1)


def high_low(row):
    high = row.astype(bf16).astype(f32)
    return jnp.concatenate(
        [high, row - high, jnp.zeros((6, row.shape[1]), f32)], axis=0
    ).astype(bf16)


def column_of(square):
    count = square.shape[0]
    padded = jnp.concatenate([square, jnp.zeros((LANES - count, LANES), f32)], axis=0)
    turned = padded.T
    return jnp.concatenate([turned[:, i : i + 1] for i in range(count)], axis=0)


def make_kernel(n_proto, n_rows, rows, patches, protos):
    all_rows = float(rows * n_rows)
    all_protos = float(protos * n_proto)
    keep = protos // n_rows
    row_tiles = rows // LANES
    proto_tiles = protos // LANES
    keep_tiles = keep // LANES
    half = rows // 2
    pairs = n_proto // 2
    chunk = D // pairs
    others = n_rows - 1

    def kernel(
        sp_any, tp_any, idx_ref, w_any, rc_ref,
        loss_ref, gp_ref, gw_ref,
        sp_ref, tp_ref, w_ref,
        onehot, wh, wht, plan, expo, tt, srt, sht, scaled, part, csum, vbuf,
        cbuf, rbuf, r3buf, fbuf,
        ot, os, planx, cpart,
        asend, arecv, axs, axr, bsend, brecv, bxs, bxr, dfull,
        in_s, y_s, y_r, p_s, p_r, f_s, f_r,
        gy_s, gy_r, gz_s, gz_r, gc_s, gc_r,
        s_s, s_r, x_s, x_r,
    ):
        p = lax.axis_index("proto")
        y = lax.axis_index("rows")
        pair = lax.div(p, 2)
        core = lax.rem(p, 2)

        barrier = pltpu.get_barrier_semaphore()

        def greet(d, carry):
            pl.semaphore_signal(
                barrier, inc=1, device_id=(lax.rem(p + d, n_proto), y), device_id_type=MESH
            )
            return carry

        for d in range(1, n_rows):
            pl.semaphore_signal(
                barrier, inc=1, device_id=(p, lax.rem(y + d, n_rows)), device_id_type=MESH
            )
        lax.fori_loop(1, n_proto, greet, 0)

        fetch_t = pltpu.make_async_copy(tp_any, tp_ref, in_s.at[0])
        fetch_w = pltpu.make_async_copy(w_any, w_ref, in_s.at[1])
        fetch_s = pltpu.make_async_copy(sp_any, sp_ref, in_s.at[2])
        fetch_t.start()
        fetch_w.start()
        fetch_s.start()

        def remote(source, target, send, recv, device):
            return pltpu.make_async_remote_copy(
                src_ref=source, dst_ref=target, send_sem=send, recv_sem=recv,
                device_id=device, device_id_type=MESH,
            )

        def to_plane(d):
            return (lax.rem(p + d, n_proto), y)

        def to_core(d):
            return (lax.rem(p + 2 * d, n_proto), y)

        def to_row(d):
            return (p, lax.rem(y + d, n_rows))

        sibling = (p + 1 - 2 * core, y)

        def each(count, copy_of, act):
            def body(d, carry):
                act(copy_of(d))
                return carry

            lax.fori_loop(1, count, body, 0)

        def start(copy):
            copy.start()

        def wait(copy):
            copy.wait()

        def totals(buf, e):
            return lambda d: remote(buf.at[p], buf.at[p], p_s.at[e, d], p_r.at[e, d], to_plane(d))

        def columns(e):
            return lambda d: remote(
                cbuf.at[e, y], cbuf.at[e, y], y_s.at[e, d], y_r.at[e, d], to_row(d)
            )

        def factors(e):
            return lambda d: remote(
                fbuf.at[e, y], fbuf.at[e, y], f_s.at[e, d], f_r.at[e, d], to_row(d)
            )

        def row_each(copy_of, act):
            for d in range(1, n_rows):
                act(copy_of(d))

        def sum_slots(buf, count):
            total = buf[0].astype(f32)
            for i in range(1, count):
                total = total + buf[i].astype(f32)
            return total

        features = pl.ds(pl.multiple_of(pair * chunk, chunk), chunk)
        my_half = pl.ds(pl.multiple_of(core * half, half), half)
        other_half = pl.ds(pl.multiple_of((1 - core) * half, half), half)

        def group_row(e, own, far):
            return lambda d: remote(
                own.at[features, my_half], far.at[d - 1, features, my_half],
                gy_s.at[e, d], gy_r.at[e, d], to_row(d),
            )

        def group_core(e, far):
            piece = far.at[:, features, my_half]
            return lambda d: remote(piece, piece, gz_s.at[e, d], gz_r.at[e, d], to_core(d))

        def group_pair(e, far):
            piece = far.at[:, :, my_half]
            return remote(piece, piece, gc_s.at[e], gc_r.at[e], sibling)

        idx_row = unfold(idx_ref[...])
        for i in range(patches // BLOCK):
            spot = lax.broadcasted_iota(jnp.int32, (BLOCK, rows), 0) + i * BLOCK
            onehot[i * BLOCK : (i + 1) * BLOCK, :] = (spot == idx_row).astype(bf16)
        fetch_t.wait()
        teacher = dot(tp_ref[...], onehot[...], TN)
        tt[...] = (
            teacher * lax.rsqrt(jnp.sum(teacher * teacher, axis=0, keepdims=True) + epsilon)
        ).astype(bf16)

        ones = jnp.ones((8, LANES), bf16)
        fetch_w.wait()

        def plan_block(i, carry):
            at = pl.ds(pl.multiple_of(i * WIDE, WIDE), WIDE)
            block = w_ref[at, :].astype(f32)
            scale = lax.rsqrt(jnp.sum(block * block, axis=1, keepdims=True) + epsilon)
            unit = (block * scale).astype(bf16)
            wh[at, :] = unit
            wht[:, at] = unit.T
            values = jnp.exp(dot(unit, tt[...], NN) * (1.0 / teacher_temp))
            plan[at, :] = values.astype(bf16)
            lane_sum = values[:, :LANES]
            for j in range(1, row_tiles):
                lane_sum = lane_sum + values[:, j * LANES : (j + 1) * LANES]
            high = lane_sum.astype(bf16)
            low = (lane_sum - high.astype(f32)).astype(bf16)
            csum[:, at] = dot(ones, high, NT) + dot(ones, low, NT)
            return carry

        lax.fori_loop(0, protos // WIDE, plan_block, 0, unroll=2)
        pl.semaphore_wait(barrier, n_proto - 1 + n_rows - 1)

        def columns_begin(e, sums):
            cbuf[e, y] = fold(sums)
            row_each(columns(e), start)

        def columns_end(e):
            row_each(columns(e), wait)
            total = cbuf[e, 0]
            for i in range(1, n_rows):
                total = total + cbuf[e, i]
            return 1.0 / (all_protos * total)

        def row_sums(v):
            sums = dot(high_low(unfold(v)), plan[...], NN)
            return fold(sums[0:1, :] + sums[1:2, :])

        def column_sums(u):
            sums = dot(high_low(unfold(u)), plan[...], NT)
            return sums[0:1, :] + sums[1:2, :]

        def student_block(i, carry):
            at = pl.ds(pl.multiple_of(i * WIDE, WIDE), WIDE)
            values = jnp.exp(dot(wh[at, :], sht[...], NN) * (1.0 / student_temp))
            expo[at, :] = values.astype(bf16)
            return carry + jnp.sum(values.reshape(WIDE // 8, 8, rows), axis=0)

        columns_begin(0, csum[0:1, :])
        row_each(group_row(0, tt, ot), start)
        fetch_s.wait()
        student = dot(sp_ref[...], onehot[...], TN)
        scale_s = lax.rsqrt(jnp.sum(student * student, axis=0, keepdims=True) + epsilon)
        srt[...] = student.astype(bf16)
        sht[...] = (student * scale_s).astype(bf16)
        row_each(group_row(1, sht, os), start)
        v = columns_end(0)
        rbuf[0, p] = row_sums(v)
        each(n_proto, totals(rbuf.at[0], 0), start)
        row_each(group_row(0, tt, ot), wait)
        each(pairs, group_core(0, ot), start)
        expo_rows = lax.fori_loop(
            0, protos // WIDE, student_block, jnp.zeros((8, rows), f32), unroll=2
        )
        rbuf[2, p] = fold(jnp.sum(expo_rows, axis=0, keepdims=True))
        each(n_proto, totals(rbuf.at[0], 0), wait)
        u = 1.0 / (all_rows * sum_slots(rbuf.at[0], n_proto))

        columns_begin(1, column_sums(u))
        part[...] = dot(wht[...], expo[...], NN)

        def fold_pair(xs, xr, e):
            xs[...] = part[:, other_half].astype(bf16)
            return remote(xs, xr, x_s.at[e], x_r.at[e], sibling)

        def fold_core(send, recv, e):
            return lambda d: remote(
                send.at[lax.rem(pair + d, pairs)], recv.at[pair],
                s_s.at[e, d], s_r.at[e, d], to_core(d),
            )

        def fold_begin(xr, send, recv, e):
            total = part[:, my_half] + xr[...].astype(f32)
            send[...] = total.reshape(pairs, chunk, half).astype(bf16)
            recv[pair] = send[pair]
            each(pairs, fold_core(send, recv, e), start)

        a_pair = fold_pair(axs, axr, 0)
        a_pair.start()
        v = columns_end(1)
        rbuf[1, p] = row_sums(v)
        each(n_proto, totals(rbuf.at[1], 1), start)
        each(n_proto, totals(rbuf.at[2], 2), start)
        each(pairs, group_core(0, ot), wait)
        t_pair = group_pair(0, ot)
        t_pair.start()
        row_each(group_row(1, sht, os), wait)
        each(pairs, group_core(1, os), start)
        a_pair.wait()
        fold_begin(axr, asend, arecv, 0)
        t_pair.wait()
        def quarter(d):
            return pl.ds(pl.multiple_of(lax.rem(y + d, n_rows) * keep, keep), keep)

        mine = quarter(0)
        for d in range(others):
            values = jnp.exp(dot(wh[mine, :], ot[d], NN) * (1.0 / teacher_temp))
            planx[d] = values.astype(bf16)
        each(n_proto, totals(rbuf.at[1], 1), wait)
        u = 1.0 / (all_rows * sum_slots(rbuf.at[1], n_proto))

        columns_begin(2, column_sums(u))
        each(n_proto, totals(rbuf.at[2], 2), wait)
        expo_total = sum_slots(rbuf.at[2], n_proto)
        cot = rc_ref[...] * (1.0 / student_temp)
        over_expo = cot / expo_total
        fbuf[0, y] = over_expo
        row_each(factors(0), start)
        each(pairs, group_core(1, os), wait)
        s_pair = group_pair(1, os)
        s_pair.start()
        each(pairs, fold_core(asend, arecv, 0), wait)
        v = columns_end(2)
        vbuf[...] = v
        part[...] = dot((wht[...].astype(f32) * unfold(v)).astype(bf16), plan[...], NN)
        b_pair = fold_pair(bxs, bxr, 1)
        b_pair.start()
        r3buf[p] = jnp.concatenate(
            [
                row_sums(v),
                fold(jnp.sum(part[...] * sht[...].astype(f32), axis=0, keepdims=True)),
            ],
            axis=0,
        )
        each(n_proto, totals(r3buf, 3), start)
        b_pair.wait()
        fold_begin(bxr, bsend, brecv, 1)

        s_pair.wait()
        row_each(factors(0), wait)
        for d in range(others):
            values = jnp.exp(dot(wh[mine, :], os[d], NN) * (1.0 / student_temp))
            expo[quarter(d + 1), :] = values.astype(bf16)

        def contract(own, far, e):
            scaled[0] = (sht[...].astype(f32) * unfold(fbuf[e, y])).astype(bf16)
            total = dot(own[mine, :], scaled[0], NT)
            for d in range(1, n_rows):
                factor = unfold(fbuf[e, lax.rem(y + n_rows - d, n_rows)])
                scaled[d] = (os[d - 1].astype(f32) * factor).astype(bf16)
                total = total + dot(far(d), scaled[d], NT)
            return total

        cpart[...] = contract(expo, lambda d: expo[quarter(d), :], 0)
        each(n_proto, totals(r3buf, 3), wait)
        both = sum_slots(r3buf, n_proto)
        inverse = 1.0 / both[:row_tiles]
        loss_ref[:row_tiles] = jnp.log(expo_total)
        loss_ref[row_tiles:] = both[row_tiles:] * inverse * (1.0 / student_temp)
        over_rows = cot * inverse
        fbuf[1, y] = over_rows
        row_each(factors(1), start)

        a_total = sum_slots(arecv, pairs)
        each(pairs, fold_core(bsend, brecv, 1), wait)
        b_total = sum_slots(brecv, pairs)

        def half_row(square):
            row = unfold(square)
            return jnp.where(core == 0, row[:, :half], row[:, half:])

        dfull[features, my_half] = (
            a_total * half_row(over_expo) - b_total * half_row(over_rows)
        ).astype(bf16)
        own_piece = dfull.at[features, my_half]
        spread = lambda d: remote(own_piece, own_piece, s_s.at[2, d], s_r.at[2, d], to_core(d))
        each(pairs, spread, start)

        row_each(factors(1), wait)
        column = column_of(vbuf[pl.ds(pl.multiple_of(y * keep_tiles, keep_tiles), keep_tiles), :])
        total = cpart[...] - column * contract(plan, lambda d: planx[d - 1], 1)
        kept = w_ref[mine, :].astype(f32)
        scale_w = lax.rsqrt(jnp.sum(kept * kept, axis=1, keepdims=True) + epsilon)
        unit_w = kept * scale_w
        gw_ref[...] = (
            (total - unit_w * jnp.sum(unit_w * total, axis=1, keepdims=True)) * scale_w
        ).astype(bf16)

        each(pairs, spread, wait)
        my_pieces = dfull.at[:, my_half]
        d_pair = remote(my_pieces, my_pieces, x_s.at[2], x_r.at[2], sibling)
        d_pair.start()
        d_pair.wait()
        grad_unit = dfull[...].astype(f32)
        unit = srt[...].astype(f32) * scale_s
        grad_rows = (
            grad_unit - unit * jnp.sum(unit * grad_unit, axis=0, keepdims=True)
        ) * scale_s
        gp_ref[...] = dot(onehot[...], grad_rows.astype(bf16), NT).astype(bf16)

    scratch = [
        pltpu.VMEM((patches, D), bf16),
        pltpu.VMEM((patches, D), bf16),
        pltpu.VMEM((protos, D), bf16),
        pltpu.VMEM((patches, rows), bf16),
        pltpu.VMEM((protos, D), bf16),
        pltpu.VMEM((D, protos), bf16),
        pltpu.VMEM((protos, rows), bf16),
        pltpu.VMEM((protos, rows), bf16),
        pltpu.VMEM((D, rows), bf16),
        pltpu.VMEM((D, rows), bf16),
        pltpu.VMEM((D, rows), bf16),
        pltpu.VMEM((n_rows, D, rows), bf16),
        pltpu.VMEM((D, rows), f32),
        pltpu.VMEM((8, protos), f32),
        pltpu.VMEM((proto_tiles, LANES), f32),
        pltpu.VMEM((3, n_rows, proto_tiles, LANES), f32),
        pltpu.VMEM((3, n_proto, row_tiles, LANES), f32),
        pltpu.VMEM((n_proto, 2 * row_tiles, LANES), f32),
        pltpu.VMEM((2, n_rows, row_tiles, LANES), f32),
        pltpu.VMEM((others, D, rows), bf16),
        pltpu.VMEM((others, D, rows), bf16),
        pltpu.VMEM((others, keep, rows), bf16),
        pltpu.VMEM((keep, D), f32),
        pltpu.VMEM((pairs, chunk, half), bf16),
        pltpu.VMEM((pairs, chunk, half), bf16),
        pltpu.VMEM((D, half), bf16),
        pltpu.VMEM((D, half), bf16),
        pltpu.VMEM((pairs, chunk, half), bf16),
        pltpu.VMEM((pairs, chunk, half), bf16),
        pltpu.VMEM((D, half), bf16),
        pltpu.VMEM((D, half), bf16),
        pltpu.VMEM((D, rows), bf16),
        pltpu.SemaphoreType.DMA((3,)),
        pltpu.SemaphoreType.DMA((3, n_rows)),
        pltpu.SemaphoreType.DMA((3, n_rows)),
        pltpu.SemaphoreType.DMA((4, n_proto)),
        pltpu.SemaphoreType.DMA((4, n_proto)),
        pltpu.SemaphoreType.DMA((2, n_rows)),
        pltpu.SemaphoreType.DMA((2, n_rows)),
        pltpu.SemaphoreType.DMA((2, n_rows)),
        pltpu.SemaphoreType.DMA((2, n_rows)),
        pltpu.SemaphoreType.DMA((2, pairs)),
        pltpu.SemaphoreType.DMA((2, pairs)),
        pltpu.SemaphoreType.DMA((2,)),
        pltpu.SemaphoreType.DMA((2,)),
        pltpu.SemaphoreType.DMA((3, pairs)),
        pltpu.SemaphoreType.DMA((3, pairs)),
        pltpu.SemaphoreType.DMA((3,)),
        pltpu.SemaphoreType.DMA((3,)),
    ]
    return kernel, scratch


def shards(student_patches, teacher_patches, mask_index, proto_weight, row_cotangent):
    n_proto, n_rows = lax.axis_size("proto"), lax.axis_size("rows")
    rows = mask_index.shape[0]
    patches = student_patches.shape[0]
    protos = proto_weight.shape[0]
    kernel, scratch = make_kernel(n_proto, n_rows, rows, patches, protos)
    vmem = pl.BlockSpec(memory_space=pltpu.VMEM)
    anywhere = pl.BlockSpec(memory_space=pl.ANY)
    terms, grad_patches, grad_weight = pl.pallas_call(
        kernel,
        out_shape=(
            jax.ShapeDtypeStruct((2 * rows // LANES, LANES), f32),
            jax.ShapeDtypeStruct((patches, D), bf16),
            jax.ShapeDtypeStruct((protos // n_rows, D), bf16),
        ),
        in_specs=[anywhere, anywhere, vmem, anywhere, vmem],
        out_specs=(vmem, vmem, vmem),
        scratch_shapes=scratch,
        compiler_params=pltpu.CompilerParams(
            collective_id=0, has_side_effects=True, vmem_limit_bytes=60 << 20
        ),
    )(
        student_patches,
        teacher_patches,
        mask_index.reshape(rows // LANES, LANES),
        proto_weight,
        row_cotangent.reshape(rows // LANES, LANES),
    )
    tiles = rows // LANES
    loss = (terms[:tiles] - terms[tiles:]).reshape(rows)
    return loss, grad_patches.astype(f32), grad_weight.astype(f32)


def solution(mesh):
    in_specs = (P("rows", None), P("rows", None), P("rows"), P("proto", None), P("rows"))
    out_specs = (P("rows"), P("rows", None), P(("proto", "rows"), None))
    return jax.shard_map(shards, mesh=mesh, in_specs=in_specs, out_specs=out_specs, check_vma=False)
```

time: 529 us -> 86.1 us (0.16)
  blocking collectives: 301 us -> 0 us
  waiting for transfers between devices: 87.5 us -> 0 us
  Pallas kernels: 0 us -> 80.1 us
  other arithmetic: 75.5 us -> 5.09 us
  matrix products: 36.6 us -> 0 us
  between operations: 15.6 us -> 0.65 us
  local copies, waits for them, and re-layouts: 12 us -> 0.01 us
    psum x7 -> x0, blocking collectives: 301 us -> none  [the longest x3 201 us: shards(): totals = lax.psum(jnp.sum(current, axis=1), 'proto')]
    psum x1 -> x0, waiting for transfers between devices: 87.5 us -> none  [shards(): lax.psum(jnp.dot(grad_scores, weight_half, preferred_element_type=jnp.flo...]
    pallas_call x0 -> x1, Pallas kernels: none -> 80.1 us  [shards(): pl.pallas_call(kernel, out_shape=(jax.ShapeDtypeStruct((2 * rows // LANES...]
    reduce_sum x9 -> x0, other arithmetic: 45.1 us -> none  [the longest x3 22.7 us: shards(): totals = lax.psum(jnp.sum(current, axis=1), 'proto')]
    dot_general x4 -> x0, matrix products: 36.6 us -> none  [the longest x2 25.6 us: contract_last(): lax.dot_general(left_side, right_side, (((1,), (1,)), ((), ())), preferre...]
    convert_element_type x1 -> x2, other arithmetic: 15 us -> 3.75 us  [shards(): return (loss, grad_patches.astype(f32), grad_weight.astype(f32))]
    gather x2 -> x0, local copies, waits for them, and re-layouts: 8.76 us -> none  [the longest x1 4.82 us: shards(): jnp.take(student_patches, mask_index, axis=0).astype(jnp.float32)]
    scatter-add x1 -> x0, other arithmetic: 8.21 us -> none  [shards(): grad_patches = jnp.zeros((student_patches.shape[0], student_patches.shape...]
  transfers between devices with their start and end apart: 2 -> 0, of which waited for: 1 -> 0; matrix products, arithmetic and copies ran while one was open for 4% -> 0% of each run, Pallas kernels for 0% -> 0%
where the time goes in v1:
time: 86.1 us; the launch traced here: 85.9 us
  Pallas kernels  80.1 us (93%)
  other arithmetic  5.09 us (6%)
    pallas_call x1, Pallas kernels, shards(): pl.pallas_call(kernel, out_shape=(jax.ShapeDtypeStruct((2 * rows // LANES...  80.1 us
    convert_element_type x2, other arithmetic, shards(): return (loss, grad_patches.astype(f32), grad_weight.astype(f32))  3.75 us

profile of v1, /device:TPU:1, one launch (start us, length us, event | category | flops | bytes accessed | tf_op | source)
XLA Modules:
  0.0 85.9 jit_solution(2915999434465366925)
XLA Ops:
  0.6 80.1 %shard_map.76 = (f32[16,128]{1,0:T(8,128)}, bf16[2048,256]{1,0:T(8,128)(2,1)}, bf16[1024,256]{1,0:T(8,128)(2,1)}) custom-call(bf16[2048,256]{1,0:T(8,128)(2,1)} %sp_any.1, bf16[2048,256]{1,0:T(8,128)(2,1)} %tp_any.1, s32[8,128]{1,0:T(8,128)} %bitcast.4, bf16[4096,256]{1,0:T(8,128)(2,1)} %w_any.1, f32[8,128]{1,0:T(8,128)} %bitcast.5), custom_call_target="tpu_custom_call" | custom-call | tf_op jit(solution)/shard_map/pallas_call | solution.py:444
  80.8 0.0 copy-start
  80.8 1.3 %subtract_bitcast_fusion = f32[1024]{0:T(1024)} fusion(f32[16,128]{1,0:T(8,128)} %get-tuple-element.6), kind=kLoop, calls=%fused_computation | loop fusion | flops 1024 | bytes 12288 | tf_op jit(solution)/shard_map/reshape | solution.py:465
  82.1 2.7 %convert_element_type.6 = f32[2048,256]{1,0:T(8,128)} convert(bf16[2048,256]{1,0:T(8,128)(2,1)} %get-tuple-element.7) | non-fusion elementwise | flops 524288 | bytes 3145728 | tf_op jit(solution)/shard_map/convert_element_type | solution.py:466
  84.8 0.0 copy-done
  84.8 1.0 %convert_element_type.7 = f32[1024,256]{1,0:T(8,128)} convert(bf16[1024,256]{1,0:T(8,128)(2,1)S(1)} %copy-done) | non-fusion elementwise | flops 262144 | bytes 1572864 | tf_op jit(solution)/shard_map/convert_element_type | solution.py:466
Async XLA Ops:
  80.8 4.1 %copy-start = (bf16[1024,256]{1,0:T(8,128)(2,1)S(1)}, bf16[1024,256]{1,0:T(8,128)(2,1)}, u32[]{:S(2)}) copy-start(bf16[1024,256]{1,0:T(8,128)(2,1)} %get-tuple-element.8) | copy-start | bytes 1572868

commit v2 on v1

v2 whole, which is shorter than its diff:
```python
import itertools
import math

import jax
import jax.numpy as jnp
from jax import lax
from jax.experimental import pallas as pl
from jax.experimental.pallas import tpu as pltpu
from jax.sharding import PartitionSpec as P

teacher_temp = 0.07
student_temp = 0.1
epsilon = 1e-06

f32, bf16 = jnp.float32, jnp.bfloat16
MESH = pl.DeviceIdType.MESH
NN = (((1,), (0,)), ((), ()))
NT = (((1,), (1,)), ((), ()))
TN = (((0,), (0,)), ((), ()))

D = 256
LANES = 128
BLOCK = 256
WIDE = 512


def dot(left, right, dims):
    return lax.dot_general(left, right, dims, preferred_element_type=f32)


def fold(row):
    count = row.shape[1] // LANES
    return jnp.concatenate([row[:, i * LANES : (i + 1) * LANES] for i in range(count)], axis=0)


def unfold(square):
    return jnp.concatenate([square[i : i + 1, :] for i in range(square.shape[0])], axis=1)


def high_low(row):
    high = row.astype(bf16).astype(f32)
    return jnp.concatenate(
        [high, row - high, jnp.zeros((6, row.shape[1]), f32)], axis=0
    ).astype(bf16)


def column_of(square):
    count = square.shape[0]
    padded = jnp.concatenate([square, jnp.zeros((LANES - count, LANES), f32)], axis=0)
    turned = padded.T
    return jnp.concatenate([turned[:, i : i + 1] for i in range(count)], axis=0)


def make_kernel(n_proto, n_rows, rows, patches, protos):
    all_rows = float(rows * n_rows)
    all_protos = float(protos * n_proto)
    keep = protos // n_rows
    row_tiles = rows // LANES
    proto_tiles = protos // LANES
    keep_tiles = keep // LANES
    half = rows // 2
    pairs = n_proto // 2
    chunk = D // pairs
    others = n_rows - 1
    side = math.isqrt(pairs)
    assert side * side == pairs and rows == keep

    def hops(offset):
        return sum(min(step, side - step) for step in offset[:2])

    every = itertools.product(range(side), range(side), range(2))
    plane_offsets = sorted((o for o in every if any(o)), key=hops, reverse=True)
    core_offsets = [o for o in plane_offsets if o[2] == 0]
    row_offsets = sorted(range(1, n_rows), key=lambda d: -min(d, n_rows - d))

    def kernel(
        sp_any, tp_any, idx_ref, w_any, rc_ref,
        loss_ref, gr_ref, gw_ref,
        sp_ref, tp_ref, w_ref,
        shared, wh, wht, plan, expo, tt, srt, sht, scaled, part, csum, vbuf,
        cbuf, rbuf, r3buf, fbuf,
        ot, os, cpart,
        asend, arecv, axs, axr, bsend, brecv, bxs, bxr, dfull,
        in_s, y_s, y_r, p_s, p_r, f_s, f_r,
        gy_s, gy_r, gz_s, gz_r, gc_s, gc_r,
        s_s, s_r, x_s, x_r,
    ):
        p = lax.axis_index("proto")
        y = lax.axis_index("rows")
        pair = lax.div(p, 2)
        core = lax.rem(p, 2)
        z = lax.div(pair, side)
        x = lax.rem(pair, side)

        def pair_at(offset):
            return lax.rem(z + offset[0], side) * side + lax.rem(x + offset[1], side)

        def in_plane(offset):
            return (pair_at(offset) * 2 + lax.rem(core + offset[2], 2), y)

        def to_row(d):
            return (p, lax.rem(y + d, n_rows))

        sibling = (p + 1 - 2 * core, y)

        barrier = pltpu.get_barrier_semaphore()
        for offset in plane_offsets:
            pl.semaphore_signal(
                barrier, inc=1, device_id=in_plane(offset), device_id_type=MESH
            )
        for d in range(1, n_rows):
            pl.semaphore_signal(barrier, inc=1, device_id=to_row(d), device_id_type=MESH)

        fetch_t = pltpu.make_async_copy(tp_any, tp_ref, in_s.at[0])
        fetch_w = pltpu.make_async_copy(w_any, w_ref, in_s.at[1])
        fetch_s = pltpu.make_async_copy(sp_any, sp_ref, in_s.at[2])
        fetch_t.start()
        fetch_w.start()
        fetch_s.start()

        def remote(source, target, send, recv, device):
            return pltpu.make_async_remote_copy(
                src_ref=source, dst_ref=target, send_sem=send, recv_sem=recv,
                device_id=device, device_id_type=MESH,
            )

        def arrived(landing, send, recv):
            pltpu.make_async_copy(landing, landing, recv).wait()
            pltpu.make_async_copy(landing, landing, send).wait()

        def totals_begin(buf, e):
            for offset in plane_offsets:
                remote(buf.at[p], buf.at[p], p_s.at[e], p_r.at[e], in_plane(offset)).start()

        def totals_end(buf, e):
            arrived(buf.at[pl.ds(0, n_proto - 1)], p_s.at[e], p_r.at[e])

        def rows_begin(buf, send, recv):
            for d in row_offsets:
                remote(buf.at[y], buf.at[y], send, recv, to_row(d)).start()

        def rows_end(buf, send, recv):
            arrived(buf.at[pl.ds(0, others)], send, recv)

        def sum_slots(buf, count):
            total = buf[0].astype(f32)
            for i in range(1, count):
                total = total + buf[i].astype(f32)
            return total

        features = pl.ds(pl.multiple_of(pair * chunk, chunk), chunk)
        my_half = pl.ds(pl.multiple_of(core * half, half), half)
        other_half = pl.ds(pl.multiple_of((1 - core) * half, half), half)
        all_but_one = pl.ds(0, (pairs - 1) * chunk)

        def group_row_begin(e, own, far):
            for d in row_offsets:
                remote(
                    own.at[features, my_half], far.at[d - 1, features, my_half],
                    gy_s.at[e], gy_r.at[e], to_row(d),
                ).start()

        def group_row_end(e, far):
            arrived(far.at[:, features, my_half], gy_s.at[e], gy_r.at[e])

        def group_core_begin(e, far):
            piece = far.at[:, features, my_half]
            for offset in core_offsets:
                remote(piece, piece, gz_s.at[e], gz_r.at[e], in_plane(offset)).start()

        def group_core_end(e, far):
            arrived(far.at[:, all_but_one, my_half], gz_s.at[e], gz_r.at[e])

        def group_pair(e, far):
            piece = far.at[:, :, my_half]
            return remote(piece, piece, gc_s.at[e], gc_r.at[e], sibling)

        idx_row = unfold(idx_ref[...])
        for i in range(patches // rows):
            spot = lax.broadcasted_iota(jnp.int32, (rows, rows), 0) + i * rows
            shared[i] = (spot == idx_row).astype(bf16)

        def masked(patch_ref):
            total = dot(patch_ref[:rows, :], shared[0], TN)
            for i in range(1, patches // rows):
                total = total + dot(patch_ref[i * rows : (i + 1) * rows, :], shared[i], TN)
            return total

        fetch_t.wait()
        teacher = masked(tp_ref)
        tt[...] = (
            teacher * lax.rsqrt(jnp.sum(teacher * teacher, axis=0, keepdims=True) + epsilon)
        ).astype(bf16)

        ones = jnp.ones((8, LANES), bf16)
        fetch_w.wait()

        def plan_block(i, carry):
            at = pl.ds(pl.multiple_of(i * WIDE, WIDE), WIDE)
            block = w_ref[at, :].astype(f32)
            scale = lax.rsqrt(jnp.sum(block * block, axis=1, keepdims=True) + epsilon)
            unit = (block * scale).astype(bf16)
            wh[at, :] = unit
            wht[:, at] = unit.T
            values = jnp.exp(dot(unit, tt[...], NN) * (1.0 / teacher_temp))
            plan[at, :] = values.astype(bf16)
            lane_sum = values[:, :LANES]
            for j in range(1, row_tiles):
                lane_sum = lane_sum + values[:, j * LANES : (j + 1) * LANES]
            high = lane_sum.astype(bf16)
            low = (lane_sum - high.astype(f32)).astype(bf16)
            csum[:, at] = dot(ones, high, NT) + dot(ones, low, NT)
            return carry

        lax.fori_loop(0, protos // WIDE, plan_block, 0, unroll=2)
        pl.semaphore_wait(barrier, n_proto - 1 + n_rows - 1)

        def columns_begin(e, sums):
            cbuf[e, y] = fold(sums)
            rows_begin(cbuf.at[e], y_s.at[e], y_r.at[e])

        def columns_end(e):
            rows_end(cbuf.at[e], y_s.at[e], y_r.at[e])
            total = cbuf[e, 0]
            for i in range(1, n_rows):
                total = total + cbuf[e, i]
            return 1.0 / (all_protos * total)

        def row_sums(v):
            sums = dot(high_low(unfold(v)), plan[...], NN)
            return fold(sums[0:1, :] + sums[1:2, :])

        def column_sums(u):
            parts = high_low(unfold(u))
            sums = jnp.concatenate(
                [dot(parts, shared[i], NN) for i in range(n_rows)], axis=1
            )
            return sums[0:1, :] + sums[1:2, :]

        def turn(i, carry):
            at = pl.ds(pl.multiple_of(i * BLOCK, BLOCK), BLOCK)
            to = pl.ds(pl.multiple_of(lax.rem(i, keep // BLOCK) * BLOCK, BLOCK), BLOCK)
            shared[lax.div(i, keep // BLOCK), :, to] = plan[at, :].T
            return carry

        turns = protos // BLOCK

        def student_block(i, carry):
            at = pl.ds(pl.multiple_of(i * WIDE, WIDE), WIDE)
            values = jnp.exp(dot(wh[at, :], sht[...], NN) * (1.0 / student_temp))
            expo[at, :] = values.astype(bf16)
            return carry + jnp.sum(values.reshape(WIDE // 8, 8, rows), axis=0)

        columns_begin(0, csum[0:1, :])
        group_row_begin(0, tt, ot)
        fetch_s.wait()
        student = masked(sp_ref)
        scale_s = lax.rsqrt(jnp.sum(student * student, axis=0, keepdims=True) + epsilon)
        srt[...] = student.astype(bf16)
        sht[...] = (student * scale_s).astype(bf16)
        lax.fori_loop(0, turns // 2, turn, 0, unroll=2)
        v = columns_end(0)
        rbuf[0, p] = row_sums(v)
        totals_begin(rbuf.at[0], 0)
        group_row_begin(1, sht, os)
        expo_rows = lax.fori_loop(
            0, protos // WIDE, student_block, jnp.zeros((8, rows), f32), unroll=2
        )
        lax.fori_loop(turns // 2, turns, turn, 0, unroll=2)
        rbuf[2, p] = fold(jnp.sum(expo_rows, axis=0, keepdims=True))
        totals_end(rbuf.at[0], 0)
        u = 1.0 / (all_rows * sum_slots(rbuf.at[0], n_proto))

        columns_begin(1, column_sums(u))
        group_row_end(0, ot)
        group_core_begin(0, ot)
        part[...] = dot(wht[...], expo[...], NN)

        def fold_pair(xs, xr, e):
            xs[...] = part[:, other_half].astype(bf16)
            return remote(xs, xr, x_s.at[e], x_r.at[e], sibling)

        def fold_begin(xr, send, recv, e):
            total = part[:, my_half] + xr[...].astype(f32)
            send[...] = total.reshape(pairs, chunk, half).astype(bf16)
            for offset in core_offsets:
                remote(
                    send.at[pair_at(offset)], recv.at[pair], s_s.at[e], s_r.at[e],
                    in_plane(offset),
                ).start()
            recv[pair] = send[pair]

        def fold_end(recv, e):
            arrived(recv.at[pl.ds(0, pairs - 1)], s_s.at[e], s_r.at[e])
            return sum_slots(recv, pairs)

        a_pair = fold_pair(axs, axr, 0)
        a_pair.start()
        v = columns_end(1)
        rbuf[1, p] = row_sums(v)
        totals_begin(rbuf.at[1], 1)
        totals_begin(rbuf.at[2], 2)
        group_core_end(0, ot)
        t_pair = group_pair(0, ot)
        t_pair.start()
        group_row_end(1, os)
        totals_end(rbuf.at[1], 1)
        u = 1.0 / (all_rows * sum_slots(rbuf.at[1], n_proto))

        columns_begin(2, column_sums(u))
        group_core_begin(1, os)
        a_pair.wait()
        fold_begin(axr, asend, arecv, 0)
        totals_end(rbuf.at[2], 2)
        expo_total = sum_slots(rbuf.at[2], n_proto)
        cot = rc_ref[...] * (1.0 / student_temp)
        over_expo = cot / expo_total
        fbuf[0, y] = over_expo
        rows_begin(fbuf.at[0], f_s.at[0], f_r.at[0])

        def quarter(d):
            return pl.ds(pl.multiple_of(lax.rem(y + d, n_rows) * keep, keep), keep)

        mine = quarter(0)
        t_pair.wait()
        for d in range(others):
            values = jnp.exp(dot(wh[mine, :], ot[d], NN) * (1.0 / teacher_temp))
            shared[d] = values.astype(bf16)
        v = columns_end(2)
        vbuf[...] = v
        part[...] = dot((wht[...].astype(f32) * unfold(v)).astype(bf16), plan[...], NN)
        b_pair = fold_pair(bxs, bxr, 1)
        b_pair.start()
        r3buf[p] = jnp.concatenate(
            [
                row_sums(v),
                fold(jnp.sum(part[...] * sht[...].astype(f32), axis=0, keepdims=True)),
            ],
            axis=0,
        )
        totals_begin(r3buf, 3)
        b_pair.wait()
        fold_begin(bxr, bsend, brecv, 1)

        group_core_end(1, os)
        s_pair = group_pair(1, os)
        s_pair.start()
        s_pair.wait()
        rows_end(fbuf.at[0], f_s.at[0], f_r.at[0])
        for d in range(others):
            values = jnp.exp(dot(wh[mine, :], os[d], NN) * (1.0 / student_temp))
            expo[quarter(d + 1), :] = values.astype(bf16)

        def contract(own, far, e):
            scaled[0] = (sht[...].astype(f32) * unfold(fbuf[e, y])).astype(bf16)
            total = dot(own[mine, :], scaled[0], NT)
            for d in range(1, n_rows):
                factor = unfold(fbuf[e, lax.rem(y + n_rows - d, n_rows)])
                scaled[d] = (os[d - 1].astype(f32) * factor).astype(bf16)
                total = total + dot(far(d), scaled[d], NT)
            return total

        cpart[...] = contract(expo, lambda d: expo[quarter(d), :], 0)
        totals_end(r3buf, 3)
        both = sum_slots(r3buf, n_proto)
        inverse = 1.0 / both[:row_tiles]
        loss_ref[:row_tiles] = jnp.log(expo_total)
        loss_ref[row_tiles:] = both[row_tiles:] * inverse * (1.0 / student_temp)
        over_rows = cot * inverse
        fbuf[1, y] = over_rows
        rows_begin(fbuf.at[1], f_s.at[1], f_r.at[1])

        a_total = fold_end(arecv, 0)
        b_total = fold_end(brecv, 1)

        def half_row(square):
            row = unfold(square)
            return jnp.where(core == 0, row[:, :half], row[:, half:])

        dfull[features, my_half] = (
            a_total * half_row(over_expo) - b_total * half_row(over_rows)
        ).astype(bf16)
        own_piece = dfull.at[features, my_half]
        for offset in core_offsets:
            remote(own_piece, own_piece, s_s.at[2], s_r.at[2], in_plane(offset)).start()

        rows_end(fbuf.at[1], f_s.at[1], f_r.at[1])
        column = column_of(vbuf[pl.ds(pl.multiple_of(y * keep_tiles, keep_tiles), keep_tiles), :])
        total = cpart[...] - column * contract(plan, lambda d: shared[d - 1], 1)
        kept = w_ref[mine, :].astype(f32)
        scale_w = lax.rsqrt(jnp.sum(kept * kept, axis=1, keepdims=True) + epsilon)
        unit_w = kept * scale_w
        gw_ref[...] = (
            (total - unit_w * jnp.sum(unit_w * total, axis=1, keepdims=True)) * scale_w
        ).astype(bf16)

        arrived(dfull.at[all_but_one, my_half], s_s.at[2], s_r.at[2])
        my_pieces = dfull.at[:, my_half]
        d_pair = remote(my_pieces, my_pieces, x_s.at[2], x_r.at[2], sibling)
        d_pair.start()
        d_pair.wait()
        grad_unit = dfull[...].astype(f32)
        unit = srt[...].astype(f32) * scale_s
        gr_ref[...] = (
            (grad_unit - unit * jnp.sum(unit * grad_unit, axis=0, keepdims=True)) * scale_s
        ).astype(bf16)

    scratch = [
        pltpu.VMEM((patches, D), bf16),
        pltpu.VMEM((patches, D), bf16),
        pltpu.VMEM((protos, D), bf16),
        pltpu.VMEM((n_rows, rows, keep), bf16),
        pltpu.VMEM((protos, D), bf16),
        pltpu.VMEM((D, protos), bf16),
        pltpu.VMEM((protos, rows), bf16),
        pltpu.VMEM((protos, rows), bf16),
        pltpu.VMEM((D, rows), bf16),
        pltpu.VMEM((D, rows), bf16),
        pltpu.VMEM((D, rows), bf16),
        pltpu.VMEM((n_rows, D, rows), bf16),
        pltpu.VMEM((D, rows), f32),
        pltpu.VMEM((8, protos), f32),
        pltpu.VMEM((proto_tiles, LANES), f32),
        pltpu.VMEM((3, n_rows, proto_tiles, LANES), f32),
        pltpu.VMEM((3, n_proto, row_tiles, LANES), f32),
        pltpu.VMEM((n_proto, 2 * row_tiles, LANES), f32),
        pltpu.VMEM((2, n_rows, row_tiles, LANES), f32),
        pltpu.VMEM((others, D, rows), bf16),
        pltpu.VMEM((others, D, rows), bf16),
        pltpu.VMEM((keep, D), f32),
        pltpu.VMEM((pairs, chunk, half), bf16),
        pltpu.VMEM((pairs, chunk, half), bf16),
        pltpu.VMEM((D, half), bf16),
        pltpu.VMEM((D, half), bf16),
        pltpu.VMEM((pairs, chunk, half), bf16),
        pltpu.VMEM((pairs, chunk, half), bf16),
        pltpu.VMEM((D, half), bf16),
        pltpu.VMEM((D, half), bf16),
        pltpu.VMEM((D, rows), bf16),
        pltpu.SemaphoreType.DMA((3,)),
        pltpu.SemaphoreType.DMA((3,)),
        pltpu.SemaphoreType.DMA((3,)),
        pltpu.SemaphoreType.DMA((4,)),
        pltpu.SemaphoreType.DMA((4,)),
        pltpu.SemaphoreType.DMA((2,)),
        pltpu.SemaphoreType.DMA((2,)),
        pltpu.SemaphoreType.DMA((2,)),
        pltpu.SemaphoreType.DMA((2,)),
        pltpu.SemaphoreType.DMA((2,)),
        pltpu.SemaphoreType.DMA((2,)),
        pltpu.SemaphoreType.DMA((2,)),
        pltpu.SemaphoreType.DMA((2,)),
        pltpu.SemaphoreType.DMA((3,)),
        pltpu.SemaphoreType.DMA((3,)),
        pltpu.SemaphoreType.DMA((3,)),
        pltpu.SemaphoreType.DMA((3,)),
    ]
    return kernel, scratch


def finish(idx_ref, terms_ref, gr_ref, gw_in, loss_ref, gp_ref, gw_ref):
    step = pl.program_id(0)
    here, rows = gp_ref.shape[0], gr_ref.shape[1]
    spot = lax.broadcasted_iota(jnp.int32, (here, rows), 0) + step * here
    onehot = (spot == unfold(idx_ref[...])).astype(bf16)
    gp_ref[...] = dot(onehot, gr_ref[...], NT)
    gw_ref[...] = gw_in[...].astype(f32)
    tiles = loss_ref.shape[0]
    loss_ref[...] = terms_ref[:tiles] - terms_ref[tiles:]


def shards(student_patches, teacher_patches, mask_index, proto_weight, row_cotangent):
    n_proto, n_rows = lax.axis_size("proto"), lax.axis_size("rows")
    rows = mask_index.shape[0]
    patches = student_patches.shape[0]
    protos = proto_weight.shape[0]
    kernel, scratch = make_kernel(n_proto, n_rows, rows, patches, protos)
    vmem = pl.BlockSpec(memory_space=pltpu.VMEM)
    anywhere = pl.BlockSpec(memory_space=pl.ANY)
    squares = mask_index.reshape(rows // LANES, LANES)
    terms, grad_rows, grad_kept = pl.pallas_call(
        kernel,
        out_shape=(
            jax.ShapeDtypeStruct((2 * rows // LANES, LANES), f32),
            jax.ShapeDtypeStruct((D, rows), bf16),
            jax.ShapeDtypeStruct((protos // n_rows, D), bf16),
        ),
        in_specs=[anywhere, anywhere, vmem, anywhere, vmem],
        out_specs=(vmem, vmem, vmem),
        scratch_shapes=scratch,
        compiler_params=pltpu.CompilerParams(
            collective_id=0, has_side_effects=True, vmem_limit_bytes=60 << 20
        ),
    )(
        student_patches,
        teacher_patches,
        squares,
        proto_weight,
        row_cotangent.reshape(rows // LANES, LANES),
    )
    tiles = rows // LANES
    steps = 4
    loss, grad_patches, grad_weight = pl.pallas_call(
        finish,
        grid=(steps,),
        out_shape=(
            jax.ShapeDtypeStruct((tiles, LANES), f32),
            jax.ShapeDtypeStruct((patches, D), f32),
            jax.ShapeDtypeStruct((protos // n_rows, D), f32),
        ),
        in_specs=[
            pl.BlockSpec((tiles, LANES), lambda i: (0, 0)),
            pl.BlockSpec((2 * tiles, LANES), lambda i: (0, 0)),
            pl.BlockSpec((D, rows), lambda i: (0, 0)),
            pl.BlockSpec((protos // n_rows // steps, D), lambda i: (i, 0)),
        ],
        out_specs=(
            pl.BlockSpec((tiles, LANES), lambda i: (0, 0)),
            pl.BlockSpec((patches // steps, D), lambda i: (i, 0)),
            pl.BlockSpec((protos // n_rows // steps, D), lambda i: (i, 0)),
        ),
        compiler_params=pltpu.CompilerParams(vmem_limit_bytes=60 << 20),
    )(squares, terms, grad_rows, grad_kept)
    return loss.reshape(rows), grad_patches, grad_weight


def solution(mesh):
    in_specs = (P("rows", None), P("rows", None), P("rows"), P("proto", None), P("rows"))
    out_specs = (P("rows"), P("rows", None), P(("proto", "rows"), None))
    return jax.shard_map(shards, mesh=mesh, in_specs=in_specs, out_specs=out_specs, check_vma=False)
```

time: 86.1 us -> 76.8 us (0.89)
  other arithmetic: 5.09 us -> 0 us
  Pallas kernels: 80.1 us -> 75.9 us
    pallas_call x1, Pallas kernels: 80.1 us -> 71.2 us  [shards(): pl.pallas_call(kernel, out_shape=(jax.ShapeDtypeStruct((2 * rows // LANES...]
    pallas_call x0 -> x1, Pallas kernels: none -> 4.69 us  [shards(): pl.pallas_call(finish, grid=(steps,), out_shape=(jax.ShapeDtypeStruct((ti...]
    convert_element_type x2 -> x0, other arithmetic: 3.75 us -> none  [shards(): return (loss, grad_patches.astype(f32), grad_weight.astype(f32))]
    reshape x1 -> x0, other arithmetic: 1.34 us -> none  [shards(): loss = (terms[:tiles] - terms[tiles:]).reshape(rows)]
where the time goes in v2:
time: 76.8 us; the launch traced here: 76.6 us
  Pallas kernels  75.9 us (99%)
    pallas_call x1, Pallas kernels, shards(): pl.pallas_call(kernel, out_shape=(jax.ShapeDtypeStruct((2 * rows // LANES...  71.2 us
    pallas_call x1, Pallas kernels, shards(): pl.pallas_call(finish, grid=(steps,), out_shape=(jax.ShapeDtypeStruct((ti...  4.69 us

profile of v2, /device:TPU:1, one launch (start us, length us, event | category | flops | bytes accessed | tf_op | source)
XLA Modules:
  0.0 76.6 jit_solution(10028016947294257452)
XLA Ops:
  0.6 71.2 %shard_map.76 = (f32[16,128]{1,0:T(8,128)}, bf16[256,1024]{1,0:T(8,128)(2,1)}, bf16[1024,256]{1,0:T(8,128)(2,1)}) custom-call(bf16[2048,256]{1,0:T(8,128)(2,1)} %sp_any.1, bf16[2048,256]{1,0:T(8,128)(2,1)} %tp_any.1, s32[8,128]{1,0:T(8,128)} %bitcast.3, bf16[4096,256]{1,0:T(8,128)(2,1)} %w_any.1, f32[8,128]{1,0:T(8,128)} %bitcast.5), custom_call_target="tpu_custom_call" | custom-call | tf_op jit(solution)/shard_map/pallas_call | solution.py:481
  71.9 4.7 %shard_map.77 = (f32[8,128]{1,0:T(8,128)}, f32[2048,256]{1,0:T(8,128)}, f32[1024,256]{1,0:T(8,128)}) custom-call(s32[8,128]{1,0:T(8,128)} %bitcast.4, f32[16,128]{1,0:T(8,128)} %get-tuple-element.9.terms_ref, bf16[256,1024]{1,0:T(8,128)(2,1)} %get-tuple-element.10.gr_ref, bf16[1024,256]{1,0:T(8,128)(2,1)} %get-tuple-element.11.gw_in), custom_call_target="tpu_custom_call" | custom-call | tf_op jit(solution)/shard_map/pallas_call | solution.py:503

commit v3 on v2

--- a/solution.py
+++ b/solution.py
@@ -62,6 +62,7 @@
     pairs = n_proto // 2
     chunk = D // pairs
     others = n_rows - 1
+    half_tiles = proto_tiles // 2
     side = math.isqrt(pairs)
     assert side * side == pairs and rows == keep
 
@@ -71,6 +72,8 @@
     every = itertools.product(range(side), range(side), range(2))
     plane_offsets = sorted((o for o in every if any(o)), key=hops, reverse=True)
     core_offsets = [o for o in plane_offsets if o[2] == 0]
+    line_offsets = sorted(range(1, side), key=lambda d: -min(d, side - d))
+    share = D // side
     row_offsets = sorted(range(1, n_rows), key=lambda d: -min(d, n_rows - d))
 
     def kernel(
@@ -78,7 +81,7 @@
         loss_ref, gr_ref, gw_ref,
         sp_ref, tp_ref, w_ref,
         shared, wh, wht, plan, expo, tt, srt, sht, scaled, part, csum, vbuf,
-        cbuf, rbuf, r3buf, fbuf,
+        cbuf, rbuf, fbuf,
         ot, os, cpart,
         asend, arecv, axs, axr, bsend, brecv, bxs, bxr, dfull,
         in_s, y_s, y_r, p_s, p_r, f_s, f_r,
@@ -153,23 +156,27 @@
         other_half = pl.ds(pl.multiple_of((1 - core) * half, half), half)
         all_but_one = pl.ds(0, (pairs - 1) * chunk)
 
+        def carried(e):
+            return pl.ds(pl.multiple_of((x, z)[e] * share, share), share)
+
         def group_row_begin(e, own, far):
             for d in row_offsets:
                 remote(
-                    own.at[features, my_half], far.at[d - 1, features, my_half],
+                    own.at[carried(e), my_half], far.at[d - 1, carried(e), my_half],
                     gy_s.at[e], gy_r.at[e], to_row(d),
                 ).start()
 
         def group_row_end(e, far):
-            arrived(far.at[:, features, my_half], gy_s.at[e], gy_r.at[e])
+            arrived(far.at[:, carried(e), my_half], gy_s.at[e], gy_r.at[e])
 
         def group_core_begin(e, far):
-            piece = far.at[:, features, my_half]
-            for offset in core_offsets:
+            piece = far.at[:, carried(e), my_half]
+            for step in line_offsets:
+                offset = ((0, step, 0), (step, 0, 0))[e]
                 remote(piece, piece, gz_s.at[e], gz_r.at[e], in_plane(offset)).start()
 
         def group_core_end(e, far):
-            arrived(far.at[:, all_but_one, my_half], gz_s.at[e], gz_r.at[e])
+            arrived(far.at[:, pl.ds(0, D - share), my_half], gz_s.at[e], gz_r.at[e])
 
         def group_pair(e, far):
             piece = far.at[:, :, my_half]
@@ -215,27 +222,49 @@
         lax.fori_loop(0, protos // WIDE, plan_block, 0, unroll=2)
         pl.semaphore_wait(barrier, n_proto - 1 + n_rows - 1)
 
-        def columns_begin(e, sums):
-            cbuf[e, y] = fold(sums)
-            rows_begin(cbuf.at[e], y_s.at[e], y_r.at[e])
-
-        def columns_end(e):
-            rows_end(cbuf.at[e], y_s.at[e], y_r.at[e])
-            total = cbuf[e, 0]
+        def columns_half(h):
+            return pl.ds(h * half_tiles, half_tiles)
+
+        def columns_begin(e, sums_of):
+            for h in range(2):
+                cbuf[e, y, columns_half(h), :] = fold(sums_of(h))
+                mine_here = cbuf.at[e, y, columns_half(h)]
+                for d in row_offsets:
+                    remote(
+                        mine_here, mine_here, y_s.at[e, h], y_r.at[e, h], to_row(d)
+                    ).start()
+
+        def columns_end(e, h):
+            here = columns_half(h)
+            arrived(cbuf.at[e, pl.ds(0, others), here], y_s.at[e, h], y_r.at[e, h])
+            total = cbuf[e, 0, here, :]
             for i in range(1, n_rows):
-                total = total + cbuf[e, i]
+                total = total + cbuf[e, i, here, :]
             return 1.0 / (all_protos * total)
 
-        def row_sums(v):
-            sums = dot(high_low(unfold(v)), plan[...], NN)
-            return fold(sums[0:1, :] + sums[1:2, :])
+        def plan_half(h):
+            return plan[h * (protos // 2) : (h + 1) * (protos // 2), :]
+
+        def both_rows(sums):
+            return sums[0:1, :] + sums[1:2, :]
+
+        def row_sums(e):
+            sums = jnp.zeros((8, rows), f32)
+            for h in range(2):
+                v = columns_end(e, h)
+                vbuf[h * half_tiles : (h + 1) * half_tiles, :] = v
+                sums = sums + dot(high_low(unfold(v)), plan_half(h), NN)
+            return fold(both_rows(sums))
 
         def column_sums(u):
             parts = high_low(unfold(u))
-            sums = jnp.concatenate(
-                [dot(parts, shared[i], NN) for i in range(n_rows)], axis=1
-            )
-            return sums[0:1, :] + sums[1:2, :]
+            slots = n_rows // 2
+
+            def sums_of(h):
+                sums = [dot(parts, shared[h * slots + i], NN) for i in range(slots)]
+                return both_rows(jnp.concatenate(sums, axis=1))
+
+            return sums_of
 
         def turn(i, carry):
             at = pl.ds(pl.multiple_of(i * BLOCK, BLOCK), BLOCK)
@@ -251,7 +280,7 @@
             expo[at, :] = values.astype(bf16)
             return carry + jnp.sum(values.reshape(WIDE // 8, 8, rows), axis=0)
 
-        columns_begin(0, csum[0:1, :])
+        columns_begin(0, lambda h: csum[0:1, h * (protos // 2) : (h + 1) * (protos // 2)])
         group_row_begin(0, tt, ot)
         fetch_s.wait()
         student = masked(sp_ref)
@@ -259,22 +288,24 @@
         srt[...] = student.astype(bf16)
         sht[...] = (student * scale_s).astype(bf16)
         lax.fori_loop(0, turns // 2, turn, 0, unroll=2)
-        v = columns_end(0)
-        rbuf[0, p] = row_sums(v)
+        rbuf[0, p] = row_sums(0)
         totals_begin(rbuf.at[0], 0)
         group_row_begin(1, sht, os)
+        early = protos // WIDE // 2
         expo_rows = lax.fori_loop(
-            0, protos // WIDE, student_block, jnp.zeros((8, rows), f32), unroll=2
+            0, early, student_block, jnp.zeros((8, rows), f32), unroll=2
         )
         lax.fori_loop(turns // 2, turns, turn, 0, unroll=2)
-        rbuf[2, p] = fold(jnp.sum(expo_rows, axis=0, keepdims=True))
         totals_end(rbuf.at[0], 0)
         u = 1.0 / (all_rows * sum_slots(rbuf.at[0], n_proto))
 
         columns_begin(1, column_sums(u))
         group_row_end(0, ot)
         group_core_begin(0, ot)
-        part[...] = dot(wht[...], expo[...], NN)
+        group_row_end(1, os)
+        group_core_begin(1, os)
+        expo_rows = lax.fori_loop(early, protos // WIDE, student_block, expo_rows, unroll=2)
+        rbuf[2, p] = fold(jnp.sum(expo_rows, axis=0, keepdims=True))
 
         def fold_pair(xs, xr, e):
             xs[...] = part[:, other_half].astype(bf16)
@@ -294,21 +325,22 @@
             arrived(recv.at[pl.ds(0, pairs - 1)], s_s.at[e], s_r.at[e])
             return sum_slots(recv, pairs)
 
+        rbuf[1, p] = row_sums(1)
+        totals_begin(rbuf.at[1], 1)
+        totals_begin(rbuf.at[2], 2)
+        part[...] = dot(wht[...], expo[...], NN)
         a_pair = fold_pair(axs, axr, 0)
         a_pair.start()
-        v = columns_end(1)
-        rbuf[1, p] = row_sums(v)
-        totals_begin(rbuf.at[1], 1)
-        totals_begin(rbuf.at[2], 2)
         group_core_end(0, ot)
         t_pair = group_pair(0, ot)
         t_pair.start()
-        group_row_end(1, os)
+        group_core_end(1, os)
+        s_pair = group_pair(1, os)
+        s_pair.start()
         totals_end(rbuf.at[1], 1)
         u = 1.0 / (all_rows * sum_slots(rbuf.at[1], n_proto))
 
         columns_begin(2, column_sums(u))
-        group_core_begin(1, os)
         a_pair.wait()
         fold_begin(axr, asend, arecv, 0)
         totals_end(rbuf.at[2], 2)
@@ -326,50 +358,43 @@
         for d in range(others):
             values = jnp.exp(dot(wh[mine, :], ot[d], NN) * (1.0 / teacher_temp))
             shared[d] = values.astype(bf16)
-        v = columns_end(2)
-        vbuf[...] = v
-        part[...] = dot((wht[...].astype(f32) * unfold(v)).astype(bf16), plan[...], NN)
+        rbuf[3, p] = row_sums(2)
+        totals_begin(rbuf.at[3], 3)
+        for h in range(2):
+            v_row = unfold(vbuf[h * half_tiles : (h + 1) * half_tiles, :])
+            here = wht[:, h * (protos // 2) : (h + 1) * (protos // 2)].astype(f32)
+            piece = dot((here * v_row).astype(bf16), plan_half(h), NN)
+            part[...] = piece if h == 0 else part[...] + piece
         b_pair = fold_pair(bxs, bxr, 1)
         b_pair.start()
-        r3buf[p] = jnp.concatenate(
-            [
-                row_sums(v),
-                fold(jnp.sum(part[...] * sht[...].astype(f32), axis=0, keepdims=True)),
-            ],
-            axis=0,
-        )
-        totals_begin(r3buf, 3)
+        rbuf[4, p] = fold(jnp.sum(part[...] * sht[...].astype(f32), axis=0, keepdims=True))
         b_pair.wait()
         fold_begin(bxr, bsend, brecv, 1)
-
-        group_core_end(1, os)
-        s_pair = group_pair(1, os)
-        s_pair.start()
+        totals_begin(rbuf.at[4], 4)
+
         s_pair.wait()
-        rows_end(fbuf.at[0], f_s.at[0], f_r.at[0])
         for d in range(others):
             values = jnp.exp(dot(wh[mine, :], os[d], NN) * (1.0 / student_temp))
             expo[quarter(d + 1), :] = values.astype(bf16)
 
-        def contract(own, far, e):
+        def contract_own(own, e):
             scaled[0] = (sht[...].astype(f32) * unfold(fbuf[e, y])).astype(bf16)
-            total = dot(own[mine, :], scaled[0], NT)
+            return dot(own[mine, :], scaled[0], NT)
+
+        def contract_far(total, far, e):
             for d in range(1, n_rows):
                 factor = unfold(fbuf[e, lax.rem(y + n_rows - d, n_rows)])
                 scaled[d] = (os[d - 1].astype(f32) * factor).astype(bf16)
                 total = total + dot(far(d), scaled[d], NT)
             return total
 
-        cpart[...] = contract(expo, lambda d: expo[quarter(d), :], 0)
-        totals_end(r3buf, 3)
-        both = sum_slots(r3buf, n_proto)
-        inverse = 1.0 / both[:row_tiles]
-        loss_ref[:row_tiles] = jnp.log(expo_total)
-        loss_ref[row_tiles:] = both[row_tiles:] * inverse * (1.0 / student_temp)
+        totals_end(rbuf.at[3], 3)
+        inverse = 1.0 / sum_slots(rbuf.at[3], n_proto)
         over_rows = cot * inverse
         fbuf[1, y] = over_rows
         rows_begin(fbuf.at[1], f_s.at[1], f_r.at[1])
-
+        rows_end(fbuf.at[0], f_s.at[0], f_r.at[0])
+        cpart[...] = contract_far(contract_own(expo, 0), lambda d: expo[quarter(d), :], 0)
         a_total = fold_end(arecv, 0)
         b_total = fold_end(brecv, 1)
 
@@ -384,9 +409,16 @@
         for offset in core_offsets:
             remote(own_piece, own_piece, s_s.at[2], s_r.at[2], in_plane(offset)).start()
 
+        totals_end(rbuf.at[4], 4)
+        loss_ref[:row_tiles] = jnp.log(expo_total)
+        loss_ref[row_tiles:] = (
+            sum_slots(rbuf.at[4], n_proto) * inverse * (1.0 / student_temp)
+        )
+
+        own_part = contract_own(plan, 1)
         rows_end(fbuf.at[1], f_s.at[1], f_r.at[1])
         column = column_of(vbuf[pl.ds(pl.multiple_of(y * keep_tiles, keep_tiles), keep_tiles), :])
-        total = cpart[...] - column * contract(plan, lambda d: shared[d - 1], 1)
+        total = cpart[...] - column * contract_far(own_part, lambda d: shared[d - 1], 1)
         kept = w_ref[mine, :].astype(f32)
         scale_w = lax.rsqrt(jnp.sum(kept * kept, axis=1, keepdims=True) + epsilon)
         unit_w = kept * scale_w
@@ -403,7 +435,7 @@
         unit = srt[...].astype(f32) * scale_s
         gr_ref[...] = (
             (grad_unit - unit * jnp.sum(unit * grad_unit, axis=0, keepdims=True)) * scale_s
-        ).astype(bf16)
+        ).astype(bf16).T
 
     scratch = [
         pltpu.VMEM((patches, D), bf16),
@@ -422,8 +454,7 @@
         pltpu.VMEM((8, protos), f32),
         pltpu.VMEM((proto_tiles, LANES), f32),
         pltpu.VMEM((3, n_rows, proto_tiles, LANES), f32),
-        pltpu.VMEM((3, n_proto, row_tiles, LANES), f32),
-        pltpu.VMEM((n_proto, 2 * row_tiles, LANES), f32),
+        pltpu.VMEM((5, n_proto, row_tiles, LANES), f32),
         pltpu.VMEM((2, n_rows, row_tiles, LANES), f32),
         pltpu.VMEM((others, D, rows), bf16),
         pltpu.VMEM((others, D, rows), bf16),
@@ -438,10 +469,10 @@
         pltpu.VMEM((D, half), bf16),
         pltpu.VMEM((D, rows), bf16),
         pltpu.SemaphoreType.DMA((3,)),
-        pltpu.SemaphoreType.DMA((3,)),
-        pltpu.SemaphoreType.DMA((3,)),
-        pltpu.SemaphoreType.DMA((4,)),
-        pltpu.SemaphoreType.DMA((4,)),
+        pltpu.SemaphoreType.DMA((3, 2)),
+        pltpu.SemaphoreType.DMA((3, 2)),
+        pltpu.SemaphoreType.DMA((5,)),
+        pltpu.SemaphoreType.DMA((5,)),
         pltpu.SemaphoreType.DMA((2,)),
         pltpu.SemaphoreType.DMA((2,)),
         pltpu.SemaphoreType.DMA((2,)),
@@ -460,10 +491,10 @@
 
 def finish(idx_ref, terms_ref, gr_ref, gw_in, loss_ref, gp_ref, gw_ref):
     step = pl.program_id(0)
-    here, rows = gp_ref.shape[0], gr_ref.shape[1]
+    here, rows = gp_ref.shape[0], gr_ref.shape[0]
     spot = lax.broadcasted_iota(jnp.int32, (here, rows), 0) + step * here
     onehot = (spot == unfold(idx_ref[...])).astype(bf16)
-    gp_ref[...] = dot(onehot, gr_ref[...], NT)
+    gp_ref[...] = dot(onehot, gr_ref[...], NN)
     gw_ref[...] = gw_in[...].astype(f32)
     tiles = loss_ref.shape[0]
     loss_ref[...] = terms_ref[:tiles] - terms_ref[tiles:]
@@ -482,7 +513,7 @@
         kernel,
         out_shape=(
             jax.ShapeDtypeStruct((2 * rows // LANES, LANES), f32),
-            jax.ShapeDtypeStruct((D, rows), bf16),
+            jax.ShapeDtypeStruct((rows, D), bf16),
             jax.ShapeDtypeStruct((protos // n_rows, D), bf16),
         ),
         in_specs=[anywhere, anywhere, vmem, anywhere, vmem],
@@ -499,7 +530,7 @@
         row_cotangent.reshape(rows // LANES, LANES),
     )
     tiles = rows // LANES
-    steps = 4
+    steps = 2
     loss, grad_patches, grad_weight = pl.pallas_call(
         finish,
         grid=(steps,),
@@ -511,7 +542,7 @@
         in_specs=[
             pl.BlockSpec((tiles, LANES), lambda i: (0, 0)),
             pl.BlockSpec((2 * tiles, LANES), lambda i: (0, 0)),
-            pl.BlockSpec((D, rows), lambda i: (0, 0)),
+            pl.BlockSpec((rows, D), lambda i: (0, 0)),
             pl.BlockSpec((protos // n_rows // steps, D), lambda i: (i, 0)),
         ],
         out_specs=(

time: 76.8 us -> 69.7 us (0.908)
  Pallas kernels: 75.9 us -> 68.9 us
    pallas_call x1, Pallas kernels: 71.2 us -> 65.2 us  [shards(): pl.pallas_call(kernel, out_shape=(jax.ShapeDtypeStruct((2 * rows // LANES...]
    pallas_call x1, Pallas kernels: 4.69 us -> 3.74 us  [shards(): pl.pallas_call(finish, grid=(steps,), out_shape=(jax.ShapeDtypeStruct((ti...]
where the time goes in v3:
time: 69.7 us; the launch traced here: 69.5 us
  Pallas kernels  68.9 us (99%)
    pallas_call x1, Pallas kernels, shards(): pl.pallas_call(kernel, out_shape=(jax.ShapeDtypeStruct((2 * rows // LANES...  65.2 us
    pallas_call x1, Pallas kernels, shards(): pl.pallas_call(finish, grid=(steps,), out_shape=(jax.ShapeDtypeStruct((ti...  3.74 us

profile of v3, /device:TPU:1, one launch (start us, length us, event | category | flops | bytes accessed | tf_op | source)
XLA Modules:
  0.0 69.5 jit_solution(15589207982217782017)
XLA Ops:
  0.6 65.2 %shard_map.76 = (f32[16,128]{1,0:T(8,128)}, bf16[1024,256]{1,0:T(8,128)(2,1)}, bf16[1024,256]{1,0:T(8,128)(2,1)}) custom-call(bf16[2048,256]{1,0:T(8,128)(2,1)} %sp_any.1, bf16[2048,256]{1,0:T(8,128)(2,1)} %tp_any.1, s32[8,128]{1,0:T(8,128)} %bitcast.3, bf16[4096,256]{1,0:T(8,128)(2,1)} %w_any.1, f32[8,128]{1,0:T(8,128)} %bitcast.5), custom_call_target="tpu_custom_call" | custom-call | tf_op jit(solution)/shard_map/pallas_call | solution.py:512
  65.8 3.7 %shard_map.77 = (f32[8,128]{1,0:T(8,128)}, f32[2048,256]{1,0:T(8,128)}, f32[1024,256]{1,0:T(8,128)}) custom-call(s32[8,128]{1,0:T(8,128)} %bitcast.4, f32[16,128]{1,0:T(8,128)} %get-tuple-element.9.terms_ref, bf16[1024,256]{1,0:T(8,128)(2,1)} %get-tuple-element.10.gr_ref, bf16[1024,256]{1,0:T(8,128)(2,1)} %get-tuple-element.11.gw_in), custom_call_target="tpu_custom_call" | custom-call | tf_op jit(solution)/shard_map/pallas_call | solution.py:534

commit v4 on v3

--- a/solution.py
+++ b/solution.py
@@ -64,7 +64,7 @@
     others = n_rows - 1
     half_tiles = proto_tiles // 2
     side = math.isqrt(pairs)
-    assert side * side == pairs and rows == keep
+    assert side == 4 and side * side == pairs and rows == keep
 
     def hops(offset):
         return sum(min(step, side - step) for step in offset[:2])
@@ -72,7 +72,6 @@
     every = itertools.product(range(side), range(side), range(2))
     plane_offsets = sorted((o for o in every if any(o)), key=hops, reverse=True)
     core_offsets = [o for o in plane_offsets if o[2] == 0]
-    line_offsets = sorted(range(1, side), key=lambda d: -min(d, side - d))
     share = D // side
     row_offsets = sorted(range(1, n_rows), key=lambda d: -min(d, n_rows - d))
 
@@ -156,27 +155,29 @@
         other_half = pl.ds(pl.multiple_of((1 - core) * half, half), half)
         all_but_one = pl.ds(0, (pairs - 1) * chunk)
 
-        def carried(e):
-            return pl.ds(pl.multiple_of((x, z)[e] * share, share), share)
+        def carried(e, step=0):
+            return pl.ds(pl.multiple_of(lax.rem((x, z)[e] + step, side) * share, share), share)
 
         def group_row_begin(e, own, far):
-            for d in row_offsets:
-                remote(
-                    own.at[carried(e), my_half], far.at[d - 1, carried(e), my_half],
-                    gy_s.at[e], gy_r.at[e], to_row(d),
-                ).start()
+            for step in (0, side // 2):
+                for d in row_offsets:
+                    remote(
+                        own.at[carried(e, step), my_half],
+                        far.at[d - 1, carried(e, step), my_half],
+                        gy_s.at[e], gy_r.at[e], to_row(d),
+                    ).start()
 
         def group_row_end(e, far):
-            arrived(far.at[:, carried(e), my_half], gy_s.at[e], gy_r.at[e])
+            arrived(far.at[:, pl.ds(0, 2 * share), my_half], gy_s.at[e], gy_r.at[e])
 
         def group_core_begin(e, far):
             piece = far.at[:, carried(e), my_half]
-            for step in line_offsets:
+            for step in (1, side - 1):
                 offset = ((0, step, 0), (step, 0, 0))[e]
                 remote(piece, piece, gz_s.at[e], gz_r.at[e], in_plane(offset)).start()
 
         def group_core_end(e, far):
-            arrived(far.at[:, pl.ds(0, D - share), my_half], gz_s.at[e], gz_r.at[e])
+            arrived(far.at[:, pl.ds(0, 2 * share), my_half], gz_s.at[e], gz_r.at[e])
 
         def group_pair(e, far):
             piece = far.at[:, :, my_half]
@@ -299,9 +300,9 @@
         totals_end(rbuf.at[0], 0)
         u = 1.0 / (all_rows * sum_slots(rbuf.at[0], n_proto))
 
-        columns_begin(1, column_sums(u))
         group_row_end(0, ot)
         group_core_begin(0, ot)
+        columns_begin(1, column_sums(u))
         group_row_end(1, os)
         group_core_begin(1, os)
         expo_rows = lax.fori_loop(early, protos // WIDE, student_block, expo_rows, unroll=2)

time: 69.7 us -> 67.6 us (0.970)
  Pallas kernels: 68.9 us -> 66.8 us
    pallas_call x1, Pallas kernels: 65.2 us -> 63 us  [shards(): pl.pallas_call(kernel, out_shape=(jax.ShapeDtypeStruct((2 * rows // LANES...]
where the time goes in v4:
time: 67.6 us; the launch traced here: 67.4 us
  Pallas kernels  66.8 us (99%)
    pallas_call x1, Pallas kernels, shards(): pl.pallas_call(kernel, out_shape=(jax.ShapeDtypeStruct((2 * rows // LANES...  63 us
    pallas_call x1, Pallas kernels, shards(): pl.pallas_call(finish, grid=(steps,), out_shape=(jax.ShapeDtypeStruct((ti...  3.74 us

profile of v4, /device:TPU:1, one launch (start us, length us, event | category | flops | bytes accessed | tf_op | source)
XLA Modules:
  0.0 67.4 jit_solution(14204388532148198578)
XLA Ops:
  0.6 63.0 %shard_map.76 = (f32[16,128]{1,0:T(8,128)}, bf16[1024,256]{1,0:T(8,128)(2,1)}, bf16[1024,256]{1,0:T(8,128)(2,1)}) custom-call(bf16[2048,256]{1,0:T(8,128)(2,1)} %sp_any.1, bf16[2048,256]{1,0:T(8,128)(2,1)} %tp_any.1, s32[8,128]{1,0:T(8,128)} %bitcast.3, bf16[4096,256]{1,0:T(8,128)(2,1)} %w_any.1, f32[8,128]{1,0:T(8,128)} %bitcast.5), custom_call_target="tpu_custom_call" | custom-call | tf_op jit(solution)/shard_map/pallas_call | solution.py:513
  63.7 3.7 %shard_map.77 = (f32[8,128]{1,0:T(8,128)}, f32[2048,256]{1,0:T(8,128)}, f32[1024,256]{1,0:T(8,128)}) custom-call(s32[8,128]{1,0:T(8,128)} %bitcast.4, f32[16,128]{1,0:T(8,128)} %get-tuple-element.9.terms_ref, bf16[1024,256]{1,0:T(8,128)(2,1)} %get-tuple-element.10.gr_ref, bf16[1024,256]{1,0:T(8,128)(2,1)} %get-tuple-element.11.gw_in), custom_call_target="tpu_custom_call" | custom-call | tf_op jit(solution)/shard_map/pallas_call | solution.py:535

commit v5 on v4

--- a/solution.py
+++ b/solution.py
@@ -420,6 +420,10 @@
         rows_end(fbuf.at[1], f_s.at[1], f_r.at[1])
         column = column_of(vbuf[pl.ds(pl.multiple_of(y * keep_tiles, keep_tiles), keep_tiles), :])
         total = cpart[...] - column * contract_far(own_part, lambda d: shared[d - 1], 1)
+        arrived(dfull.at[all_but_one, my_half], s_s.at[2], s_r.at[2])
+        my_pieces = dfull.at[:, my_half]
+        d_pair = remote(my_pieces, my_pieces, x_s.at[2], x_r.at[2], sibling)
+        d_pair.start()
         kept = w_ref[mine, :].astype(f32)
         scale_w = lax.rsqrt(jnp.sum(kept * kept, axis=1, keepdims=True) + epsilon)
         unit_w = kept * scale_w
@@ -427,10 +431,6 @@
             (total - unit_w * jnp.sum(unit_w * total, axis=1, keepdims=True)) * scale_w
         ).astype(bf16)
 
-        arrived(dfull.at[all_but_one, my_half], s_s.at[2], s_r.at[2])
-        my_pieces = dfull.at[:, my_half]
-        d_pair = remote(my_pieces, my_pieces, x_s.at[2], x_r.at[2], sibling)
-        d_pair.start()
         d_pair.wait()
         grad_unit = dfull[...].astype(f32)
         unit = srt[...].astype(f32) * scale_s

time: 67.6 us -> 67.6 us (level)
  no operation moved by 1% of the time
where the time goes in v5:
time: 67.6 us; the launch traced here: 67.4 us
  Pallas kernels  66.8 us (99%)
    pallas_call x1, Pallas kernels, shards(): pl.pallas_call(kernel, out_shape=(jax.ShapeDtypeStruct((2 * rows // LANES...  63 us
    pallas_call x1, Pallas kernels, shards(): pl.pallas_call(finish, grid=(steps,), out_shape=(jax.ShapeDtypeStruct((ti...  3.74 us

profile of v5, /device:TPU:1, one launch (start us, length us, event | category | flops | bytes accessed | tf_op | source)
XLA Modules:
  0.0 67.4 jit_solution(5459397402439728326)
XLA Ops:
  0.6 63.0 %shard_map.76 = (f32[16,128]{1,0:T(8,128)}, bf16[1024,256]{1,0:T(8,128)(2,1)}, bf16[1024,256]{1,0:T(8,128)(2,1)}) custom-call(bf16[2048,256]{1,0:T(8,128)(2,1)} %sp_any.1, bf16[2048,256]{1,0:T(8,128)(2,1)} %tp_any.1, s32[8,128]{1,0:T(8,128)} %bitcast.3, bf16[4096,256]{1,0:T(8,128)(2,1)} %w_any.1, f32[8,128]{1,0:T(8,128)} %bitcast.5), custom_call_target="tpu_custom_call" | custom-call | tf_op jit(solution)/shard_map/pallas_call | solution.py:513
  63.7 3.7 %shard_map.77 = (f32[8,128]{1,0:T(8,128)}, f32[2048,256]{1,0:T(8,128)}, f32[1024,256]{1,0:T(8,128)}) custom-call(s32[8,128]{1,0:T(8,128)} %bitcast.4, f32[16,128]{1,0:T(8,128)} %get-tuple-element.9.terms_ref, bf16[1024,256]{1,0:T(8,128)(2,1)} %get-tuple-element.10.gr_ref, bf16[1024,256]{1,0:T(8,128)(2,1)} %get-tuple-element.11.gw_in), custom_call_target="tpu_custom_call" | custom-call | tf_op jit(solution)/shard_map/pallas_call | solution.py:535
